TPU v7x, 32 devices: a whole 2x2x4 slice. The times are simulated.
32 devices in a mesh: clus: 16 (over z, x, core), coef: 2 (over y).
Axes of the slice: x: 2, y: 2, z: 4, core: 2. Of those that a mesh axis runs over, the one named last changes fastest.
Arguments:
- density: bfloat16 [256, 128, 256], P('clus', 'coef'), may hold values from -6 to 6
- near_list: int32 [256, 9], P('clus'), may hold values from 0 to 255, as said below
- far_list: int32 [32, 27], P('clus'), may hold values from 0 to 31
- near_blocks: bfloat16 [256, 9, 128, 128], P('clus', None, 'coef'), may hold values from -0.1875 to 0.1875
- basis: bfloat16 [256, 128, 64], P('clus', 'coef'), may hold values from -0.5 to 0.5
- transfer: bfloat16 [256, 64, 64], P('clus'), may hold values from -0.25 to 0.25
- coupling: bfloat16 [32, 27, 64, 64], P('clus', None, None, 'coef'), may hold values from -0.15625 to 0.15625
Outputs:
- first: bfloat16 [256, 128, 256], P('clus', 'coef')
- second: bfloat16 [256, 128, 256], P('clus', 'coef')
Inputs may be any that keep to these rules, and one draw needn't show every extreme that they name: near_list[i, 0] is i itself; every entry differs from its row's cluster i by at most 4, and entries i + 4 and i - 4 appear wherever they lie in range.
All inputs are finite; a program needn't handle non-finite values.
Results may differ from a plain program's by a relative error of at most 0.014.
Values may be sent and summed in bfloat16 or wider, within the bound.
A program may use at most 64 MiB of HBM per device.

v0:
```python
import jax
import jax.numpy as jnp
from jax import lax
from jax.sharding import PartitionSpec as P

CHILD = 8
NWIN = 4


def padded(block, sides, width):
    for axis, dim in sides:
        count = lax.axis_size(axis)
        forward = [(i, i + 1) for i in range(count - 1)]
        backward = [(target, source) for source, target in forward]
        low = lax.ppermute(
            lax.slice_in_dim(block, block.shape[dim] - width, None, axis=dim), axis, forward
        )
        high = lax.ppermute(lax.slice_in_dim(block, 0, width, axis=dim), axis, backward)
        block = jnp.concatenate([low, block, high], axis=dim)
    return block


def near_field(extended, near_list, near_blocks, offset):
    local = near_list - offset
    total = jnp.zeros((near_blocks.shape[0], near_blocks.shape[2], extended.shape[2]), jnp.float32)
    for column in range(near_list.shape[1]):
        picked = jnp.take(extended, local[:, column], axis=0)
        total = total + jnp.einsum(
            "cmn,cnr->cmr", near_blocks[:, column], picked, preferred_element_type=jnp.float32
        )
    return total


def lift_leaves(transfer_rows, coeffs):
    upper = coeffs.astype(jnp.bfloat16)
    lower_bits = (coeffs - upper.astype(jnp.float32)).astype(jnp.bfloat16)
    high_part = jnp.einsum("csq,csr->cqr", transfer_rows, upper, preferred_element_type=jnp.float32)
    return high_part + jnp.einsum(
        "csq,csr->cqr", transfer_rows, lower_bits, preferred_element_type=jnp.float32
    )


def far_middle(parent_part, far_list, coupling):
    parent_coef = lax.psum_scatter(
        parent_part.astype(jnp.bfloat16), "coef", scatter_dimension=1, tiled=True
    )
    piece = lax.all_gather(parent_coef, "clus", axis=0, tiled=True)
    slots = jnp.arange(piece.shape[0], dtype=jnp.int32)
    select = (far_list[:, :, None] == slots[None, None, :]).astype(jnp.bfloat16)
    picked = jnp.einsum("pkj,jqr->pkqr", select, piece, preferred_element_type=jnp.float32).astype(
        jnp.bfloat16
    )
    coupled = jnp.einsum("pkaq,pkqr->par", coupling, picked, preferred_element_type=jnp.float32)
    return lax.psum(coupled.astype(jnp.bfloat16), "coef")


def split_operator(values, near_list, far_list, near_blocks, basis, transfer, coupling):
    leaves = values.shape[0]
    vectors = values.shape[2]
    rank_full = transfer.shape[1]
    parents = leaves // CHILD
    offset = lax.axis_index("clus") * leaves - NWIN
    whole_rows = lax.all_gather(values, "coef", axis=1, tiled=True)
    extended = padded(whole_rows, (("clus", 0),), NWIN)
    near_part = near_field(extended, near_list, near_blocks, offset)
    up_part = jnp.einsum("cms,cmr->csr", basis, values, preferred_element_type=jnp.float32)
    lifted = lift_leaves(transfer, up_part)
    parent_part = jnp.sum(lifted.reshape(parents, CHILD, rank_full, vectors), axis=1)
    far_coef = far_middle(parent_part, far_list, coupling)
    grouped = transfer.reshape(parents, CHILD, rank_full, rank_full)
    lower = jnp.einsum(
        "pcsq,pqr->pcsr", grouped, far_coef, preferred_element_type=jnp.float32
    ).astype(jnp.bfloat16)
    lower = lower.reshape(leaves, rank_full, vectors)
    far_part = jnp.einsum("cms,csr->cmr", basis, lower, preferred_element_type=jnp.float32)
    return (far_part + near_part).astype(jnp.bfloat16)


def body(density, near_list, far_list, near_blocks, basis, transfer, coupling):
    first = split_operator(density, near_list, far_list, near_blocks, basis, transfer, coupling)
    second = split_operator(first, near_list, far_list, near_blocks, basis, transfer, coupling)
    return (first, second)


def solution(mesh):
    placed = (
        P("clus", "coef", None),
        P("clus", None),
        P("clus", None),
        P("clus", None, "coef", None),
        P("clus", "coef", None),
        P("clus", None, None),
        P("clus", None, None, "coef"),
    )
    return jax.shard_map(
        body,
        mesh=mesh,
        in_specs=placed,
        out_specs=(P("clus", "coef", None), P("clus", "coef", None)),
        check_vma=False,
    )
```

profile of v0, /device:TPU:3, one launch (start us, length us, event | category | flops | bytes accessed | tf_op | source)
XLA Modules:
  0.0 242.4 jit_solution(3498862999387407109)
XLA Ops:
  7.2 1.5 fusion.180
  8.8 1.3 fusion.129
  10.1 1.0 bitcast_reduce_fusion.1
  11.2 10.7 %reduce-scatter.3.cloned.1.call-done = bf16[2,32,256]{2,1,0:T(8,128)(2,1)} async-done(((bf16[2,64,256]{2,1,0:T(8,128)(2,1)}), bf16[2,32,256]{2,1,0:T(8,128)(2,1)}) %reduce-scatter.3.cloned.1.call-update) | async-done | bytes 32784 | tf_op jit(solution)/shard_map/reduce_scatter | solution.py:44
  21.9 20.4 %all_gather.12 = bf16[32,32,256]{2,1,0:T(8,128)(2,1)S(1)} all-gather(bf16[2,32,256]{2,1,0:T(8,128)(2,1)} %reduce-scatter.3.cloned.1.call-done), channel_id=1, replica_groups=mesh['clus'=16,'coef'=2] {'clus'}, dimensions={0}, use_global_device_ids=true | all-gather | bytes 557056 | tf_op jit(solution)/shard_map/all_gather | solution.py:47
  42.3 1.4 fusion.26
  45.1 18.7 %all-reduce.3.cloned.1.call-done = bf16[2,64,256]{2,1,0:T(8,128)(2,1)} async-done(((bf16[2,64,256]{2,1,0:T(8,128)(2,1)}), bf16[2,64,256]{2,1,0:T(8,128)(2,1)}) %all-reduce.3.cloned.1.call-update) | async-done | bytes 65552 | tf_op jit(solution)/shard_map/psum | solution.py:54
  63.8 1.1 convolution_convert_fusion.3
  64.9 22.2 %all-gather.3.cloned.1.call-done = bf16[16,128,256]{2,1,0:T(8,128)(2,1)} async-done(((bf16[16,64,256]{2,1,0:T(8,128)(2,1)}), bf16[16,128,256]{2,1,0:T(8,128)(2,1)}) %all-gather.3.cloned.1.call-update) | async-done | bytes 1048592 | tf_op jit(solution)/shard_map/all_gather | solution.py:63
  87.1 1.2 fusion.179
  88.3 3.7 %collective-permute-start = (bf16[4,128,256]{2,1,0:T(8,128)(2,1)S(1)}, bf16[4,128,256]{2,1,0:T(8,128)(2,1)S(1)}, u32[]{:S(2)}, u32[]{:S(2)}) collective-permute-start(bf16[4,128,256]{2,1,0:T(8,128)(2,1)S(1)} %get-tuple-element.15), channel_id=1, source_target_pairs={{0,2},{2,4},{4,6},{6,8},{8,10},{10,12},{12,14},{14,16},{16,18},{18... | collective-permute-start | bytes 786440 | tf_op jit(solution)/shard_map/ppermute | solution.py:15
  91.9 1.9 collective-permute-start.1
  93.9 1.2 fusion.181
  95.4 5.2 %collective-permute-done.1 = bf16[4,128,256]{2,1,0:T(8,128)(2,1)S(1)} collective-permute-done((bf16[4,128,256]{2,1,0:T(8,128)(2,1)S(1)}, bf16[4,128,256]{2,1,0:T(8,128)(2,1)S(1)}, u32[]{:S(2)}, u32[]{:S(2)}) %collective-permute-start.1) | collective-permute-done | bytes 262176 | tf_op jit(solution)/shard_map/ppermute | solution.py:18
  100.5 1.6 gather_fusion.8
  102.1 1.6 gather_fusion.7
  103.7 1.6 gather_fusion.6
  105.3 1.6 gather_fusion.5
  106.9 1.6 gather_fusion.4
  108.5 1.6 gather_fusion.3
  110.2 1.7 gather_fusion.2
  111.8 1.6 gather_fusion.1
  113.4 1.6 gather_fusion
  115.0 1.8 fusion.44
  117.1 1.7 fusion.46
  124.5 1.0 bitcast_reduce_fusion
  125.5 8.1 %reduce-scatter.5.cloned.1.call-done = bf16[2,32,256]{2,1,0:T(8,128)(2,1)} async-done(((bf16[2,64,256]{2,1,0:T(8,128)(2,1)}), bf16[2,32,256]{2,1,0:T(8,128)(2,1)}) %reduce-scatter.5.cloned.1.call-update) | async-done | bytes 32784 | tf_op jit(solution)/shard_map/reduce_scatter | solution.py:44
  133.6 20.4 %all_gather.14 = bf16[32,32,256]{2,1,0:T(8,128)(2,1)S(1)} all-gather(bf16[2,32,256]{2,1,0:T(8,128)(2,1)} %reduce-scatter.5.cloned.1.call-done), channel_id=1, replica_groups=mesh['clus'=16,'coef'=2] {'clus'}, dimensions={0}, use_global_device_ids=true | all-gather | bytes 557056 | tf_op jit(solution)/shard_map/all_gather | solution.py:47
  153.9 1.4 fusion.25
  156.0 19.5 %all-reduce.5.cloned.1.call-done = bf16[2,64,256]{2,1,0:T(8,128)(2,1)} async-done(((bf16[2,64,256]{2,1,0:T(8,128)(2,1)}), bf16[2,64,256]{2,1,0:T(8,128)(2,1)}) %all-reduce.5.cloned.1.call-update) | async-done | bytes 65552 | tf_op jit(solution)/shard_map/psum | solution.py:54
  175.5 1.1 convolution_convert_fusion.2
  176.6 22.6 %all-gather.5.cloned.1.call-done = bf16[16,128,256]{2,1,0:T(8,128)(2,1)} async-done(((bf16[16,64,256]{2,1,0:T(8,128)(2,1)}), bf16[16,128,256]{2,1,0:T(8,128)(2,1)}) %all-gather.5.cloned.1.call-update) | async-done | bytes 1048592 | tf_op jit(solution)/shard_map/all_gather | solution.py:63
  199.2 1.2 fusion.178
  200.4 3.7 %collective-permute-start.2 = (bf16[4,128,256]{2,1,0:T(8,128)(2,1)S(1)}, bf16[4,128,256]{2,1,0:T(8,128)(2,1)S(1)}, u32[]{:S(2)}, u32[]{:S(2)}) collective-permute-start(bf16[4,128,256]{2,1,0:T(8,128)(2,1)S(1)} %get-tuple-element.13), channel_id=1, source_target_pairs={{0,2},{2,4},{4,6},{6,8},{8,10},{10,12},{12,14},{14,16},{16,18},{18... | collective-permute-start | bytes 786440 | tf_op jit(solution)/shard_map/ppermute | solution.py:15
  204.0 2.1 collective-permute-start.3
  206.1 1.3 fusion.182
  207.5 5.1 %collective-permute-done.3 = bf16[4,128,256]{2,1,0:T(8,128)(2,1)S(1)} collective-permute-done((bf16[4,128,256]{2,1,0:T(8,128)(2,1)S(1)}, bf16[4,128,256]{2,1,0:T(8,128)(2,1)S(1)}, u32[]{:S(2)}, u32[]{:S(2)}) %collective-permute-start.3) | collective-permute-done | bytes 262176 | tf_op jit(solution)/shard_map/ppermute | solution.py:18
  212.7 1.6 gather_fusion.16
  214.2 1.6 gather_fusion.15
  215.8 1.6 gather_fusion.14
  217.4 1.6 gather_fusion.13
  219.0 1.6 gather_fusion.12
  220.6 1.6 gather_fusion.11
  222.3 1.7 gather_fusion.10
  224.6 1.6 gather_fusion.9
  226.2 1.8 fusion.29
  228.2 1.7 fusion.31
  234.0 1.5 fusion.20
  (107 shorter events, 12.9 us)
Async XLA Ops:
  7.2 35.1 %copy-start = (bf16[2,27,64,32]{2,3,1,0:T(8,128)(2,1)S(1)}, bf16[2,27,64,32]{2,3,1,0:T(8,128)(2,1)}, u32[]{:S(2)}) copy-start(bf16[2,27,64,32]{2,3,1,0:T(8,128)(2,1)} %param.15) | copy-start | bytes 663556
  7.2 2.9 %copy-start.3 = (bf16[16,64,64]{2,1,0:T(8,128)(2,1)S(1)}, bf16[16,64,64]{2,1,0:T(8,128)(2,1)}, u32[]{:S(2)}) copy-start(bf16[16,64,64]{2,1,0:T(8,128)(2,1)} %param.14) | copy-start | bytes 393220
  7.2 14.7 %reduce-scatter.3.cloned.1.call-start = ((), (), s32[]{:S(2)}) async-start(), calls=%async_computation.2 | async-start | bytes 98304 | tf_op jit(solution)/shard_map/reduce_scatter | solution.py:44
  10.1 32.2 %copy-start.24 = (s32[2,27]{1,0:T(2,128)S(1)}, s32[2,27]{1,0:T(2,128)}, u32[]{:S(2)}) copy-start(s32[2,27]{1,0:T(2,128)} %param.11) | copy-start | bytes 652
  10.1 34.4 %copy-start.23 = (s32[16,9]{1,0:T(8,128)S(1)}, s32[16,9]{1,0:T(8,128)}, u32[]{:S(2)}) copy-start(s32[16,9]{1,0:T(8,128)} %param.10) | copy-start | bytes 1732
  11.1 52.6 %all-reduce.3.cloned.1.call-start = ((), (), s32[]{:S(2)}) async-start(), calls=%async_computation.3 | async-start | bytes 131072 | tf_op jit(solution)/shard_map/psum | solution.py:54
  42.3 51.6 %copy-start.5 = (bf16[16,64,64]{2,1,0:T(8,128)(2,1)S(1)}, bf16[16,64,64]{2,1,0:T(8,128)(2,1)}, u32[]{:S(2)}) copy-start(bf16[16,64,64]{2,1,0:T(8,128)(2,1)} %param.13) | copy-start | bytes 393220
  43.8 43.3 %all-gather.3.cloned.1.call-start = ((), (), s32[]{:S(2)}) async-start(), calls=%async_computation.4 | async-start | bytes 1572864 | tf_op jit(solution)/shard_map/all_gather | solution.py:63
  44.5 89.1 %reduce-scatter.5.cloned.1.call-start = ((), (), s32[]{:S(2)}) async-start(), calls=%async_computation.5 | async-start | bytes 98304 | tf_op jit(solution)/shard_map/reduce_scatter | solution.py:44
  87.1 8.2 %copy-start.21 = (bf16[16,128,256]{2,1,0:T(8,128)(2,1)S(1)}, bf16[16,128,256]{2,1,0:T(8,128)(2,1)}, u32[]{:S(2)}) copy-start(bf16[16,128,256]{2,1,0:T(8,128)(2,1)} %all-gather.3.cloned.1.call-done) | copy-start | bytes 3145732
  88.3 7.0 %collective-permute-start = (bf16[4,128,256]{2,1,0:T(8,128)(2,1)S(1)}, bf16[4,128,256]{2,1,0:T(8,128)(2,1)S(1)}, u32[]{:S(2)}, u32[]{:S(2)}) collective-permute-start(bf16[4,128,256]{2,1,0:T(8,128)(2,1)S(1)} %get-tuple-element.15), channel_id=1, source_target_pairs={{0,2},{2,4},{4,6},{6,8},{8,10},{10,12},{12,14},{14,16},{16,18},{18... | collective-permute-start | bytes 786440 | tf_op jit(solution)/shard_map/ppermute | solution.py:15
  91.9 8.6 %collective-permute-start.1 = (bf16[4,128,256]{2,1,0:T(8,128)(2,1)S(1)}, bf16[4,128,256]{2,1,0:T(8,128)(2,1)S(1)}, u32[]{:S(2)}, u32[]{:S(2)}) collective-permute-start(bf16[4,128,256]{2,1,0:T(8,128)(2,1)S(1)} %get-tuple-element.14), channel_id=1, source_target_pairs={{2,0},{4,2},{6,4},{8,6},{10,8},{12,10},{14,12},{16,14},{18,16},{20... | collective-permute-start | bytes 786440 | tf_op jit(solution)/shard_map/ppermute | solution.py:18
  115.0 2.1 copy-start.1
  115.0 3.8 %copy-start.16 = (bf16[16,128,256]{2,1,0:T(8,128)(2,1)S(1)}, bf16[16,128,256]{2,1,0:T(8,128)(2,1)}, u32[]{:S(2)}) copy-start(bf16[16,128,256]{2,1,0:T(8,128)(2,1)} %gather_fusion.6) | copy-start | bytes 3145732
  117.1 2.1 copy-start.15
  118.8 1.2 copy-start.14
  119.2 1.3 copy-start.13
  120.0 1.3 copy-start.12
  120.5 1.3 copy-start.11
  121.3 1.3 copy-start.18
  121.3 1.6 copy-start.20
  123.7 0.8 copy-start.4
  125.5 50.0 %all-reduce.5.cloned.1.call-start = ((), (), s32[]{:S(2)}) async-start(), calls=%async_computation.6 | async-start | bytes 131072 | tf_op jit(solution)/shard_map/psum | solution.py:54
  155.4 43.8 %all-gather.5.cloned.1.call-start = ((), (), s32[]{:S(2)}) async-start(), calls=%async_computation.7 | async-start | bytes 1572864 | tf_op jit(solution)/shard_map/all_gather | solution.py:63
  199.2 8.2 %copy-start.22 = (bf16[16,128,256]{2,1,0:T(8,128)(2,1)S(1)}, bf16[16,128,256]{2,1,0:T(8,128)(2,1)}, u32[]{:S(2)}) copy-start(bf16[16,128,256]{2,1,0:T(8,128)(2,1)} %all-gather.5.cloned.1.call-done) | copy-start | bytes 3145732
  200.4 7.0 %collective-permute-start.2 = (bf16[4,128,256]{2,1,0:T(8,128)(2,1)S(1)}, bf16[4,128,256]{2,1,0:T(8,128)(2,1)S(1)}, u32[]{:S(2)}, u32[]{:S(2)}) collective-permute-start(bf16[4,128,256]{2,1,0:T(8,128)(2,1)S(1)} %get-tuple-element.13), channel_id=1, source_target_pairs={{0,2},{2,4},{4,6},{6,8},{8,10},{10,12},{12,14},{14,16},{16,18},{18... | collective-permute-start | bytes 786440 | tf_op jit(solution)/shard_map/ppermute | solution.py:15
  204.0 8.6 %collective-permute-start.3 = (bf16[4,128,256]{2,1,0:T(8,128)(2,1)S(1)}, bf16[4,128,256]{2,1,0:T(8,128)(2,1)S(1)}, u32[]{:S(2)}, u32[]{:S(2)}) collective-permute-start(bf16[4,128,256]{2,1,0:T(8,128)(2,1)S(1)} %get-tuple-element.12), channel_id=1, source_target_pairs={{2,0},{4,2},{6,4},{8,6},{10,8},{12,10},{14,12},{16,14},{18,16},{20... | collective-permute-start | bytes 786440 | tf_op jit(solution)/shard_map/ppermute | solution.py:18
  226.2 2.1 copy-start.2
  226.2 3.8 %copy-start.10 = (bf16[16,128,256]{2,1,0:T(8,128)(2,1)S(1)}, bf16[16,128,256]{2,1,0:T(8,128)(2,1)}, u32[]{:S(2)}) copy-start(bf16[16,128,256]{2,1,0:T(8,128)(2,1)} %gather_fusion.14) | copy-start | bytes 3145732
  228.2 2.1 copy-start.9
  230.0 1.2 copy-start.8
  230.4 1.3 copy-start.7
  231.2 1.3 copy-start.6
  232.5 1.2 copy-start.17
  232.5 1.5 copy-start.19
Sparse Core Ops, SparseCore 0:
  11.3 10.6 reduce-scatter.2
  43.9 19.8 all-reduce.2
  65.3 21.7 all-gather.2
  125.6 7.9 reduce-scatter.4
  155.5 19.8 all-reduce.4
  177.4 21.7 all-gather.4
where the time goes:
time: 243 us; the launch traced here: 242 us
  waiting for transfers between devices  113 us (47%)
  blocking collectives  40.7 us (17%)
  local copies, waits for them, and re-layouts  34.8 us (14%)
  matrix products  27.1 us (11%)
  between operations  14.7 us (6%)
  starting transfers between devices  11.6 us (5%)
    all_gather x2, waiting for transfers between devices, split_operator(): whole_rows = lax.all_gather(values, 'coef', axis=1, tiled=True)  44.8 us
    all_gather x2, blocking collectives, far_middle(): piece = lax.all_gather(parent_coef, 'clus', axis=0, tiled=True)  40.7 us
    psum x2, waiting for transfers between devices, far_middle(): return lax.psum(coupled.astype(jnp.bfloat16), 'coef')  38.1 us
    gather x18, local copies, waits for them, and re-layouts, near_field(): picked = jnp.take(extended, local[:, column], axis=0)  28 us
    reduce_scatter x2, waiting for transfers between devices, far_middle(): lax.psum_scatter(parent_part.astype(jnp.bfloat16), 'coef', scatter_dimens...  18.8 us
    dot_general x18, matrix products, near_field(): jnp.einsum('cmn,cnr->cmr', near_blocks[:, column], picked, preferred_elem...  14 us
    ppermute x2, waiting for transfers between devices, padded(): lax.ppermute(lax.slice_in_dim(block, 0, width, axis=dim), axis, backward)  10.3 us
    ppermute x2, starting transfers between devices, padded(): lax.ppermute(lax.slice_in_dim(block, block.shape[dim] - width, None, axis...  7.34 us
  transfers between devices with their start and end apart: 10, of which 9 were waited for; matrix products, arithmetic and copies ran while one was open for 2% of the time, Pallas kernels for 0%

commit v1 on v0

v1 whole, which is shorter than its diff:
```python
import functools

import jax
import jax.numpy as jnp
from jax import lax
from jax.experimental import pallas as pl
from jax.experimental.pallas import tpu as pltpu
from jax.sharding import PartitionSpec as P

CHILD = 8
NWIN = 4
MESH = pl.DeviceIdType.MESH
F32 = jnp.float32
BF16 = jnp.bfloat16


def kernel(
    nc, nk,
    density, near_list, far_list, nb_hbm, basis, transfer, coupling_hbm,
    first, second,
    nb, coupling, clhs, grow, ext_a, ext_b, rs_send, rs_recv, pc_a, pc_b, cp_send, cp_recv, far,
    load_sem, own_sem, y_send, y_recv, h_send, h_recv, rs_ssem, rs_rsem,
    z_ssem, z_rsem, x_ssem, x_rsem, c_ssem, c_rsem, cp_ssem, cp_rsem,
):
    leaves, rows, vectors = density.shape
    parents = leaves // CHILD
    near_k = nb.shape[1]
    far_k = coupling.shape[1]
    share = coupling.shape[3]
    rank = grow.shape[2]
    outer = nc // 4
    chunks = leaves // NWIN
    clus = lax.axis_index("clus")
    coef = lax.axis_index("coef")
    core = lax.rem(clus, 2)
    xpos = lax.rem(clus // 2, 2)
    zpos = clus // 4
    ext = (ext_a, ext_b)
    pc = (pc_a, pc_b)
    my_rows = pl.ds(pl.multiple_of(coef * rows, rows), rows)

    loads = [
        pltpu.make_async_copy(nb_hbm, nb, load_sem.at[0]),
        pltpu.make_async_copy(coupling_hbm, coupling, load_sem.at[1]),
    ]
    for load in loads:
        load.start()

    def at_coef(d):
        return lax.rem(coef + d, nk)

    def at_clus(z, x, c):
        return (z * 2 + x) * 2 + c

    def ring_z(e):
        return lax.rem(zpos + e, outer)

    barrier = pltpu.get_barrier_semaphore()

    def greet(c, k):
        pl.semaphore_signal(barrier, inc=1, device_id=(c, k), device_id_type=MESH)

    for d in range(1, nk):
        greet(clus, at_coef(d))
    for e in range(1, outer):
        greet(at_clus(ring_z(e), xpos, core), coef)
    greet(at_clus(zpos, 1 - xpos, core), coef)
    greet(at_clus(zpos, xpos, 1 - core), coef)

    @pl.when(clus > 0)
    def _():
        greet(clus - 1, coef)

    @pl.when(clus < nc - 1)
    def _():
        greet(clus + 1, coef)

    pl.semaphore_wait(
        barrier, nk + outer + jnp.minimum(clus, 1) + jnp.minimum(nc - 1 - clus, 1)
    )

    def remote(src, dst, ssem, rsem, c, k):
        return pltpu.make_async_remote_copy(
            src_ref=src, dst_ref=dst, send_sem=ssem, recv_sem=rsem,
            device_id=(c, k), device_id_type=MESH,
        )

    def y_copy(a, values, d, chunk):
        start = chunk * NWIN
        return remote(
            values.at[pl.ds(start, NWIN)],
            ext[a].at[pl.ds(NWIN + start, NWIN), my_rows],
            y_send.at[a, d, chunk], y_recv.at[a, d, chunk], clus, at_coef(d),
        )

    def halo_copy(a, values, d, up):
        lo = leaves - NWIN if up else 0
        dst_lo = 0 if up else NWIN + leaves
        owner = lax.rem(coef + nk - d, nk)
        span = pl.ds(pl.multiple_of(owner * rows, rows), rows)
        src = values.at[pl.ds(lo, NWIN)] if d == 0 else ext[a].at[pl.ds(NWIN + lo, NWIN), span]
        side = 1 if up else 0
        return remote(
            src, ext[a].at[pl.ds(dst_lo, NWIN), span],
            h_send.at[a, side, d], h_recv.at[a, side, d], clus + (1 if up else -1), coef,
        )

    def halo_start(a, values, d, up):
        @pl.when((clus < nc - 1) if up else (clus > 0))
        def _():
            halo_copy(a, values, d, up).start()

    def halo_wait_send(a, values, d, up):
        @pl.when((clus < nc - 1) if up else (clus > 0))
        def _():
            halo_copy(a, values, d, up).wait_send()

    def halo_wait_recv(a, values, d, up):
        @pl.when((clus > 0) if up else (clus < nc - 1))
        def _():
            halo_copy(a, values, d, up).wait_recv()

    def piece(a, c):
        return pc[a].at[pl.ds(c * parents, parents)]

    def z_copy(a, e):
        return remote(
            piece(a, clus), piece(a, clus), z_ssem.at[a, e], z_rsem.at[a, e],
            at_clus(ring_z(e), xpos, core), coef,
        )

    def x_copy(a, e):
        at = at_clus(ring_z(e), xpos, core)
        return remote(
            piece(a, at), piece(a, at), x_ssem.at[a, e], x_rsem.at[a, e],
            at_clus(zpos, 1 - xpos, core), coef,
        )

    def c_copy(a, f, e):
        at = at_clus(ring_z(e), xpos if f == 0 else 1 - xpos, core)
        return remote(
            piece(a, at), piece(a, at), c_ssem.at[a, f, e], c_rsem.at[a, f, e],
            at_clus(zpos, xpos, 1 - core), coef,
        )

    def rs_copy(a, d):
        to = at_coef(d)
        return remote(
            rs_send.at[a, to], rs_recv.at[a, d], rs_ssem.at[a, d], rs_rsem.at[a, d], clus, to,
        )

    def cp_copy(a, d):
        return remote(
            cp_send.at[a], cp_recv.at[a, d], cp_ssem.at[a, d], cp_rsem.at[a, d], clus, at_coef(d),
        )

    order = [0, chunks - 1] + list(range(1, chunks - 1))

    def apply_operator(a, values, result):
        own = pltpu.make_async_copy(
            values, ext[a].at[pl.ds(NWIN, leaves), my_rows], own_sem.at[a]
        )
        own.start()
        for d in range(1, nk):
            y_copy(a, values, d, order[0]).start()
        for up in (False, True):
            halo_start(a, values, 0, up)

        if a == 0:
            def combine(i, carry):
                grow[i // CHILD, pl.ds(pl.multiple_of(lax.rem(i, CHILD) * rows, rows), rows)] = jnp.dot(
                    basis[i], transfer[i], preferred_element_type=F32
                ).astype(BF16)
                return carry

            lax.fori_loop(0, leaves, combine, 0)

        parts = []
        for p in range(parents):
            mine = values[pl.ds(p * CHILD, CHILD)].reshape(CHILD * rows, vectors)
            part = lax.dot_general(
                grow[p], mine, (((0,), (0,)), ((), ())), preferred_element_type=F32
            )
            parts.append(part)
            for o in range(nk):
                rs_send[a, o, p] = part[o * share:(o + 1) * share].astype(BF16)
        for d in range(1, nk):
            rs_copy(a, d).start()
        for chunk in order[1:]:
            for d in range(1, nk):
                y_copy(a, values, d, chunk).start()

        if a == 0:
            for load in loads:
                load.wait()
            for p in range(parents):
                clhs[p] = jnp.concatenate([coupling[p, k] for k in range(far_k)], axis=1)

        total = rs_send[a, coef].astype(F32)
        for d in range(1, nk):
            rs_copy(a, d).wait_recv()
            total = total + rs_recv[a, d].astype(F32)
        pc[a][pl.ds(clus * parents, parents)] = total.astype(BF16)

        for e in range(1, outer):
            z_copy(a, e).start()
        x_copy(a, 0).start()
        c_copy(a, 0, 0).start()
        for e in range(1, outer):
            z_copy(a, outer - e).wait_recv()
            x_copy(a, e).start()
            c_copy(a, 0, e).start()
        for e in range(outer):
            x_copy(a, e).wait_recv()
            c_copy(a, 1, e).start()
        for f in range(2):
            for e in range(outer):
                c_copy(a, f, e).wait_recv()

        for up, chunk in ((False, 0), (True, chunks - 1)):
            for d in range(1, nk):
                y_copy(a, values, d, chunk).wait_recv()
                halo_start(a, values, d, up)

        for p in range(parents):
            picked = jnp.concatenate([pc[a][far_list[p, k]] for k in range(far_k)], axis=0)
            cp_send[a, p] = jnp.dot(clhs[p], picked, preferred_element_type=F32).astype(BF16)
        for d in range(1, nk):
            cp_copy(a, d).start()
        coupled = cp_send[a].astype(F32)
        for d in range(1, nk):
            cp_copy(a, d).wait_recv()
            coupled = coupled + cp_recv[a, d].astype(F32)
        coupled = coupled.astype(BF16)
        for p in range(parents):
            far[pl.ds(p * CHILD, CHILD)] = jnp.dot(
                grow[p], coupled[p], preferred_element_type=F32
            ).reshape(CHILD, rows, vectors)

        own.wait()
        for chunk in order[2:]:
            for d in range(1, nk):
                y_copy(a, values, d, chunk).wait_recv()
        for up in (False, True):
            for d in range(nk):
                halo_wait_recv(a, values, d, up)

        offset = clus * leaves - NWIN

        def near(i, carry):
            lhs = jnp.concatenate([nb[i, k] for k in range(near_k)], axis=1)
            rhs = jnp.concatenate(
                [ext[a][jnp.clip(near_list[i, k] - offset, 0, leaves + 2 * NWIN - 1)] for k in range(near_k)], axis=0
            )
            result[i] = (far[i] + jnp.dot(lhs, rhs, preferred_element_type=F32)).astype(BF16)
            return carry

        lax.fori_loop(0, leaves, near, 0)

    apply_operator(0, density, first)
    apply_operator(1, first, second)

    for a, values in ((0, density), (1, first)):
        for d in range(1, nk):
            rs_copy(a, d).wait_send()
            cp_copy(a, d).wait_send()
            for chunk in range(chunks):
                y_copy(a, values, d, chunk).wait_send()
        for up in (False, True):
            for d in range(nk):
                halo_wait_send(a, values, d, up)
        for e in range(1, outer):
            z_copy(a, e).wait_send()
        for e in range(outer):
            x_copy(a, e).wait_send()
            c_copy(a, 0, e).wait_send()
            c_copy(a, 1, e).wait_send()


def body(nc, nk, density, near_list, far_list, near_blocks, basis, transfer, coupling):
    leaves, rows, vectors = density.shape
    parents = leaves // CHILD
    rank, share = coupling.shape[2:]
    far_k = coupling.shape[1]
    outer = nc // 4
    chunks = leaves // NWIN
    vmem = pl.BlockSpec(memory_space=pltpu.VMEM)
    smem = pl.BlockSpec(memory_space=pltpu.SMEM)
    anywhere = pl.BlockSpec(memory_space=pl.ANY)
    dma = pltpu.SemaphoreType.DMA
    return pl.pallas_call(
        functools.partial(kernel, nc, nk),
        out_shape=(jax.ShapeDtypeStruct(density.shape, BF16),) * 2,
        in_specs=[vmem, smem, smem, anywhere, vmem, vmem, anywhere],
        out_specs=(vmem, vmem),
        scratch_shapes=[
            pltpu.VMEM(near_blocks.shape, BF16),
            pltpu.VMEM(coupling.shape, BF16),
            pltpu.VMEM((parents, rank, far_k * share), BF16),
            pltpu.VMEM((parents, CHILD * rows, rank), BF16),
            pltpu.VMEM((leaves + 2 * NWIN, rows * nk, vectors), BF16),
            pltpu.VMEM((leaves + 2 * NWIN, rows * nk, vectors), BF16),
            pltpu.VMEM((2, nk, parents, share, vectors), BF16),
            pltpu.VMEM((2, nk, parents, share, vectors), BF16),
            pltpu.VMEM((nc * parents, share, vectors), BF16),
            pltpu.VMEM((nc * parents, share, vectors), BF16),
            pltpu.VMEM((2, parents, rank, vectors), BF16),
            pltpu.VMEM((2, nk, parents, rank, vectors), BF16),
            pltpu.VMEM((leaves, rows, vectors), F32),
            dma((2,)),
            dma((2,)),
            dma((2, nk, chunks)),
            dma((2, nk, chunks)),
            dma((2, 2, nk)),
            dma((2, 2, nk)),
            dma((2, nk)),
            dma((2, nk)),
            dma((2, outer)),
            dma((2, outer)),
            dma((2, outer)),
            dma((2, outer)),
            dma((2, 2, outer)),
            dma((2, 2, outer)),
            dma((2, nk)),
            dma((2, nk)),
        ],
        compiler_params=pltpu.CompilerParams(
            collective_id=0, has_side_effects=True, vmem_limit_bytes=40 * 1024 * 1024
        ),
        cost_estimate=pl.CostEstimate(
            flops=4 * near_blocks.size * vectors, bytes_accessed=2 * near_blocks.size,
            transcendentals=0,
        ),
    )(density, near_list, far_list, near_blocks, basis, transfer, coupling)


def solution(mesh):
    placed = (
        P("clus", "coef", None),
        P("clus", None),
        P("clus", None),
        P("clus", None, "coef", None),
        P("clus", "coef", None),
        P("clus", None, None),
        P("clus", None, None, "coef"),
    )
    return jax.shard_map(
        functools.partial(body, mesh.shape["clus"], mesh.shape["coef"]),
        mesh=mesh,
        in_specs=placed,
        out_specs=(P("clus", "coef", None), P("clus", "coef", None)),
        check_vma=False,
    )
```

time: 243 us -> 61.1 us (0.25)
  the two profiles are of different devices: /device:TPU:3 before, /device:TPU:0 now
where the time goes in v1:
time: 61.1 us; the launch traced here: 60.8 us
  Pallas kernels  51.1 us (84%)
  local copies, waits for them, and re-layouts  8.99 us (15%)
  between operations  0.65 us (1%)
    pallas_call x1, Pallas kernels, body(): pl.pallas_call(functools.partial(kernel, nc, nk), out_shape=(jax.ShapeDty...  51.1 us
    unnamed x15, local copies, waits for them, and re-layouts  8.99 us

profile of v1, /device:TPU:0, one launch (start us, length us, event | category | flops | bytes accessed | tf_op | source)
XLA Modules:
  0.0 60.8 jit_solution(8993874516443224803)
XLA Ops:
  0.6 1.4 %copy.9.coupling_hbm = bf16[2,27,64,32]{3,2,1,0:T(8,128)(2,1)S(1)} copy(bf16[2,27,64,32]{2,3,1,0:T(8,128)(2,1)} %param.13) | data formatting | bytes 442368 | tf_op args[6]
  2.1 0.0 copy-start
  2.1 1.7 %copy-done = bf16[16,9,64,128]{3,2,1,0:T(8,128)(2,1)S(1)} copy-done((bf16[16,9,64,128]{3,2,1,0:T(8,128)(2,1)S(1)}, bf16[16,9,64,128]{3,2,1,0:T(8,128)(2,1)}, u32[]{:S(2)}) %copy-start) | copy-done | bytes 2359320
  3.7 0.0 copy-start.1
  3.7 1.0 %copy-done.1 = bf16[16,64,256]{2,1,0:T(8,128)(2,1)S(1)} copy-done((bf16[16,64,256]{2,1,0:T(8,128)(2,1)S(1)}, bf16[16,64,256]{2,1,0:T(8,128)(2,1)}, u32[]{:S(2)}) %copy-start.1) | copy-done | bytes 524312
  4.8 0.0 copy-start.2
  4.8 0.9 %copy-done.2 = bf16[16,64,64]{2,1,0:T(8,128)(2,1)S(1)} copy-done((bf16[16,64,64]{2,1,0:T(8,128)(2,1)S(1)}, bf16[16,64,64]{2,1,0:T(8,128)(2,1)}, u32[]{:S(2)}) %copy-start.2) | copy-done | bytes 131096
  5.7 0.0 copy-start.3
  5.7 0.9 %copy-done.3 = bf16[16,64,64]{2,1,0:T(8,128)(2,1)S(1)} copy-done((bf16[16,64,64]{2,1,0:T(8,128)(2,1)S(1)}, bf16[16,64,64]{2,1,0:T(8,128)(2,1)}, u32[]{:S(2)}) %copy-start.3) | copy-done | bytes 131096
  6.7 0.0 copy-start.4
  6.7 0.7 %copy-done.4 = s32[16,9]{1,0:T(8,128)S(1)} copy-done((s32[16,9]{1,0:T(8,128)S(1)}, s32[16,9]{1,0:T(8,128)}, u32[]{:S(2)}) %copy-start.4) | copy-done | bytes 600
  7.4 0.0 copy-start.5
  7.4 0.7 %copy-done.5 = s32[2,27]{1,0:T(2,128)S(1)} copy-done((s32[2,27]{1,0:T(2,128)S(1)}, s32[2,27]{1,0:T(2,128)}, u32[]{:S(2)}) %copy-start.5) | copy-done | bytes 240
  8.0 51.1 %shard_map.86 = (bf16[16,64,256]{2,1,0:T(8,128)(2,1)S(1)}, bf16[16,64,256]{2,1,0:T(8,128)(2,1)S(1)}) custom-call(bf16[16,64,256]{2,1,0:T(8,128)(2,1)S(1)} %copy-done.1, s32[16,9]{1,0:T(8,128)S(1)} %copy-done.4, s32[2,27]{1,0:T(2,128)S(1)} %copy-done.5, bf16[16,9,64,128]{3,2,1,0:T(8,128)(2,1)S(1)} %copy-done, bf16[16,64,64]{2,1,0:T(8,128)(2,1)S(1)} %copy-done.2, ...), custom_call_target="tpu_custom_call" | custom-call | flops 1207959552 | bytes 2359296 | tf_op jit(solution)/shard_map/pallas_call | solution.py:291
  59.2 0.8 %copy.12 = bf16[16,64,256]{2,1,0:T(8,128)(2,1)} copy(bf16[16,64,256]{2,1,0:T(8,128)(2,1)S(1)} %get-tuple-element.4) | data formatting | bytes 1048576
  60.0 0.8 %copy.13 = bf16[16,64,256]{2,1,0:T(8,128)(2,1)} copy(bf16[16,64,256]{2,1,0:T(8,128)(2,1)S(1)} %get-tuple-element.5) | data formatting | bytes 1048576
Async XLA Ops:
  2.1 1.7 %copy-start = (bf16[16,9,64,128]{3,2,1,0:T(8,128)(2,1)S(1)}, bf16[16,9,64,128]{3,2,1,0:T(8,128)(2,1)}, u32[]{:S(2)}) copy-start(bf16[16,9,64,128]{3,2,1,0:T(8,128)(2,1)} %nb_hbm.1) | copy-start | bytes 7077892
  3.7 1.0 %copy-start.1 = (bf16[16,64,256]{2,1,0:T(8,128)(2,1)S(1)}, bf16[16,64,256]{2,1,0:T(8,128)(2,1)}, u32[]{:S(2)}) copy-start(bf16[16,64,256]{2,1,0:T(8,128)(2,1)} %density.1) | copy-start | bytes 1572868
  4.8 0.9 %copy-start.2 = (bf16[16,64,64]{2,1,0:T(8,128)(2,1)S(1)}, bf16[16,64,64]{2,1,0:T(8,128)(2,1)}, u32[]{:S(2)}) copy-start(bf16[16,64,64]{2,1,0:T(8,128)(2,1)} %basis.1) | copy-start | bytes 393220
  5.7 0.9 %copy-start.3 = (bf16[16,64,64]{2,1,0:T(8,128)(2,1)S(1)}, bf16[16,64,64]{2,1,0:T(8,128)(2,1)}, u32[]{:S(2)}) copy-start(bf16[16,64,64]{2,1,0:T(8,128)(2,1)} %transfer.1) | copy-start | bytes 393220
  6.7 0.7 %copy-start.4 = (s32[16,9]{1,0:T(8,128)S(1)}, s32[16,9]{1,0:T(8,128)}, u32[]{:S(2)}) copy-start(s32[16,9]{1,0:T(8,128)} %near_list.1) | copy-start | bytes 1732
  7.4 0.7 %copy-start.5 = (s32[2,27]{1,0:T(2,128)S(1)}, s32[2,27]{1,0:T(2,128)}, u32[]{:S(2)}) copy-start(s32[2,27]{1,0:T(2,128)} %far_list.1) | copy-start | bytes 652

commit v2 on v1

--- a/solution.py
+++ b/solution.py
@@ -16,9 +16,10 @@
 
 def kernel(
     nc, nk,
-    density, near_list, far_list, nb_hbm, basis, transfer, coupling_hbm,
+    density_hbm, near_hbm, far_hbm, nb_hbm, basis_hbm, transfer_hbm, coupling_hbm,
     first, second,
-    nb, coupling, clhs, grow, ext_a, ext_b, rs_send, rs_recv, pc_a, pc_b, cp_send, cp_recv, far,
+    density, near_list, far_list, nb, basis, transfer, coupling,
+    clhs, grow, ext_a, ext_b, window, rs_send, rs_recv, pc_a, pc_b, cp_send, cp_recv, acc,
     load_sem, own_sem, y_send, y_recv, h_send, h_recv, rs_ssem, rs_rsem,
     z_ssem, z_rsem, x_ssem, x_rsem, c_ssem, c_rsem, cp_ssem, cp_rsem,
 ):
@@ -26,7 +27,7 @@
     parents = leaves // CHILD
     near_k = nb.shape[1]
     far_k = coupling.shape[1]
-    share = coupling.shape[3]
+    share = coupling.shape[2]
     rank = grow.shape[2]
     outer = nc // 4
     chunks = leaves // NWIN
@@ -40,8 +41,11 @@
     my_rows = pl.ds(pl.multiple_of(coef * rows, rows), rows)
 
     loads = [
-        pltpu.make_async_copy(nb_hbm, nb, load_sem.at[0]),
-        pltpu.make_async_copy(coupling_hbm, coupling, load_sem.at[1]),
+        pltpu.make_async_copy(src, dst, load_sem.at[n])
+        for n, (src, dst) in enumerate((
+            (density_hbm, density), (basis_hbm, basis), (transfer_hbm, transfer),
+            (coupling_hbm, coupling), (far_hbm, far_list), (near_hbm, near_list), (nb_hbm, nb),
+        ))
     ]
     for load in loads:
         load.start()
@@ -155,110 +159,148 @@
         )
 
     order = [0, chunks - 1] + list(range(1, chunks - 1))
-
-    def apply_operator(a, values, result):
-        own = pltpu.make_async_copy(
+    offset = clus * leaves - NWIN
+
+    def own_copy(a, values):
+        return pltpu.make_async_copy(
             values, ext[a].at[pl.ds(NWIN, leaves), my_rows], own_sem.at[a]
         )
-        own.start()
-        for d in range(1, nk):
-            y_copy(a, values, d, order[0]).start()
-        for up in (False, True):
-            halo_start(a, values, 0, up)
-
-        if a == 0:
-            def combine(i, carry):
-                grow[i // CHILD, pl.ds(pl.multiple_of(lax.rem(i, CHILD) * rows, rows), rows)] = jnp.dot(
-                    basis[i], transfer[i], preferred_element_type=F32
-                ).astype(BF16)
-                return carry
-
-            lax.fori_loop(0, leaves, combine, 0)
-
-        parts = []
+
+    def y_start(a, values, chunk):
+        for d in range(1, nk):
+            y_copy(a, values, d, chunk).start()
+
+    def y_wait(a, values, chunk):
+        for d in range(1, nk):
+            y_copy(a, values, d, chunk).wait_recv()
+
+    def near_sum(source, lo, start, count):
+        last = source.shape[0] - 1
+
+        def leaf(i, carry):
+            lhs = jnp.concatenate([nb[i, k] for k in range(near_k)], axis=1)
+            rhs = jnp.concatenate(
+                [
+                    source[jnp.clip(near_list[i, k] - offset - lo, 0, last)]
+                    for k in range(near_k)
+                ],
+                axis=0,
+            )
+            acc[i] = jnp.dot(lhs, rhs, preferred_element_type=F32)
+            return carry
+
+        lax.fori_loop(start, start + count, leaf, 0)
+
+    def lift(a, values):
         for p in range(parents):
             mine = values[pl.ds(p * CHILD, CHILD)].reshape(CHILD * rows, vectors)
             part = lax.dot_general(
                 grow[p], mine, (((0,), (0,)), ((), ())), preferred_element_type=F32
             )
-            parts.append(part)
             for o in range(nk):
                 rs_send[a, o, p] = part[o * share:(o + 1) * share].astype(BF16)
         for d in range(1, nk):
             rs_copy(a, d).start()
-        for chunk in order[1:]:
-            for d in range(1, nk):
-                y_copy(a, values, d, chunk).start()
-
-        if a == 0:
-            for load in loads:
-                load.wait()
-            for p in range(parents):
-                clhs[p] = jnp.concatenate([coupling[p, k] for k in range(far_k)], axis=1)
-
+
+    def middle(a, values):
         total = rs_send[a, coef].astype(F32)
         for d in range(1, nk):
             rs_copy(a, d).wait_recv()
             total = total + rs_recv[a, d].astype(F32)
         pc[a][pl.ds(clus * parents, parents)] = total.astype(BF16)
-
         for e in range(1, outer):
             z_copy(a, e).start()
         x_copy(a, 0).start()
         c_copy(a, 0, 0).start()
+
+        y_wait(a, values, 0)
+        for d in range(1, nk):
+            halo_start(a, values, d, False)
+
         for e in range(1, outer):
             z_copy(a, outer - e).wait_recv()
             x_copy(a, e).start()
             c_copy(a, 0, e).start()
+
+        y_wait(a, values, chunks - 1)
+        for d in range(1, nk):
+            halo_start(a, values, d, True)
+
         for e in range(outer):
             x_copy(a, e).wait_recv()
             c_copy(a, 1, e).start()
+
+        own_copy(a, values).wait()
+        y_wait(a, values, 1)
+        for d in range(nk):
+            halo_wait_recv(a, values, d, True)
+        window[...] = ext[a][pl.ds(0, 3 * NWIN)]
+        near_sum(window, 0, 0, NWIN)
+
         for f in range(2):
             for e in range(outer):
                 c_copy(a, f, e).wait_recv()
-
-        for up, chunk in ((False, 0), (True, chunks - 1)):
-            for d in range(1, nk):
-                y_copy(a, values, d, chunk).wait_recv()
-                halo_start(a, values, d, up)
-
         for p in range(parents):
             picked = jnp.concatenate([pc[a][far_list[p, k]] for k in range(far_k)], axis=0)
             cp_send[a, p] = jnp.dot(clhs[p], picked, preferred_element_type=F32).astype(BF16)
         for d in range(1, nk):
             cp_copy(a, d).start()
+
+        for chunk in range(2, chunks - 1):
+            y_wait(a, values, chunk)
+        for d in range(nk):
+            halo_wait_recv(a, values, d, False)
+        near_sum(ext[a], 0, NWIN, leaves - NWIN)
+
         coupled = cp_send[a].astype(F32)
         for d in range(1, nk):
             cp_copy(a, d).wait_recv()
             coupled = coupled + cp_recv[a, d].astype(F32)
-        coupled = coupled.astype(BF16)
-        for p in range(parents):
-            far[pl.ds(p * CHILD, CHILD)] = jnp.dot(
-                grow[p], coupled[p], preferred_element_type=F32
-            ).reshape(CHILD, rows, vectors)
-
-        own.wait()
-        for chunk in order[2:]:
-            for d in range(1, nk):
-                y_copy(a, values, d, chunk).wait_recv()
-        for up in (False, True):
-            for d in range(nk):
-                halo_wait_recv(a, values, d, up)
-
-        offset = clus * leaves - NWIN
-
-        def near(i, carry):
-            lhs = jnp.concatenate([nb[i, k] for k in range(near_k)], axis=1)
-            rhs = jnp.concatenate(
-                [ext[a][jnp.clip(near_list[i, k] - offset, 0, leaves + 2 * NWIN - 1)] for k in range(near_k)], axis=0
-            )
-            result[i] = (far[i] + jnp.dot(lhs, rhs, preferred_element_type=F32)).astype(BF16)
-            return carry
-
-        lax.fori_loop(0, leaves, near, 0)
-
-    apply_operator(0, density, first)
-    apply_operator(1, first, second)
+        return coupled.astype(BF16)
+
+    def finish(coupled, result, p):
+        far = jnp.dot(grow[p], coupled[p], preferred_element_type=F32)
+        span = pl.ds(p * CHILD, CHILD)
+        result[span] = (acc[span] + far.reshape(CHILD, rows, vectors)).astype(BF16)
+
+    loads[0].wait()
+    own_copy(0, density).start()
+    y_start(0, density, order[0])
+    for up in (False, True):
+        halo_start(0, density, 0, up)
+    for n in (1, 2):
+        loads[n].wait()
+
+    def combine(i, carry):
+        grow[i // CHILD, pl.ds(pl.multiple_of(lax.rem(i, CHILD) * rows, rows), rows)] = jnp.dot(
+            basis[i], transfer[i], preferred_element_type=F32
+        ).astype(BF16)
+        return carry
+
+    lax.fori_loop(0, leaves, combine, 0)
+    lift(0, density)
+    for chunk in order[1:]:
+        y_start(0, density, chunk)
+    for load in loads[3:]:
+        load.wait()
+    for p in range(parents):
+        clhs[p] = coupling[p].reshape(far_k * share, rank).T
+
+    coupled = middle(0, density)
+    for p in range(parents):
+        finish(coupled, first, p)
+        if p == 0:
+            y_start(1, first, order[0])
+    lift(1, first)
+    for up in (False, True):
+        halo_start(1, first, 0, up)
+    for chunk in order[1:]:
+        y_start(1, first, chunk)
+    own_copy(1, first).start()
+
+    coupled = middle(1, first)
+    for p in range(parents):
+        finish(coupled, second, p)
 
     for a, values in ((0, density), (1, first)):
         for d in range(1, nk):
@@ -278,28 +320,34 @@
 
 
 def body(nc, nk, density, near_list, far_list, near_blocks, basis, transfer, coupling):
+    coupling = jnp.swapaxes(coupling, 2, 3)
     leaves, rows, vectors = density.shape
     parents = leaves // CHILD
-    rank, share = coupling.shape[2:]
+    share, rank = coupling.shape[2:]
     far_k = coupling.shape[1]
     outer = nc // 4
     chunks = leaves // NWIN
     vmem = pl.BlockSpec(memory_space=pltpu.VMEM)
-    smem = pl.BlockSpec(memory_space=pltpu.SMEM)
     anywhere = pl.BlockSpec(memory_space=pl.ANY)
     dma = pltpu.SemaphoreType.DMA
     return pl.pallas_call(
         functools.partial(kernel, nc, nk),
         out_shape=(jax.ShapeDtypeStruct(density.shape, BF16),) * 2,
-        in_specs=[vmem, smem, smem, anywhere, vmem, vmem, anywhere],
+        in_specs=[anywhere] * 7,
         out_specs=(vmem, vmem),
         scratch_shapes=[
+            pltpu.VMEM(density.shape, BF16),
+            pltpu.SMEM(near_list.shape, jnp.int32),
+            pltpu.SMEM(far_list.shape, jnp.int32),
             pltpu.VMEM(near_blocks.shape, BF16),
+            pltpu.VMEM(basis.shape, BF16),
+            pltpu.VMEM(transfer.shape, BF16),
             pltpu.VMEM(coupling.shape, BF16),
             pltpu.VMEM((parents, rank, far_k * share), BF16),
             pltpu.VMEM((parents, CHILD * rows, rank), BF16),
             pltpu.VMEM((leaves + 2 * NWIN, rows * nk, vectors), BF16),
             pltpu.VMEM((leaves + 2 * NWIN, rows * nk, vectors), BF16),
+            pltpu.VMEM((3 * NWIN, rows * nk, vectors), BF16),
             pltpu.VMEM((2, nk, parents, share, vectors), BF16),
             pltpu.VMEM((2, nk, parents, share, vectors), BF16),
             pltpu.VMEM((nc * parents, share, vectors), BF16),
@@ -307,7 +355,7 @@
             pltpu.VMEM((2, parents, rank, vectors), BF16),
             pltpu.VMEM((2, nk, parents, rank, vectors), BF16),
             pltpu.VMEM((leaves, rows, vectors), F32),
-            dma((2,)),
+            dma((7,)),
             dma((2,)),
             dma((2, nk, chunks)),
             dma((2, nk, chunks)),
@@ -325,7 +373,7 @@
             dma((2, nk)),
         ],
         compiler_params=pltpu.CompilerParams(
-            collective_id=0, has_side_effects=True, vmem_limit_bytes=40 * 1024 * 1024
+            collective_id=0, has_side_effects=True, vmem_limit_bytes=56 * 1024 * 1024
         ),
         cost_estimate=pl.CostEstimate(
             flops=4 * near_blocks.size * vectors, bytes_accessed=2 * near_blocks.size,

time: 61.1 us -> 49.5 us (0.81)
  Pallas kernels: 51.1 us -> 44.9 us
  local copies, waits for them, and re-layouts: 8.99 us -> 3.76 us
    pallas_call x1, Pallas kernels: 51.1 us -> 44.9 us  [body(): pl.pallas_call(functools.partial(kernel, nc, nk), out_shape=(jax.ShapeDty...]
    unnamed x15 -> x2, local copies, waits for them, and re-layouts: 8.99 us -> 3.76 us
where the time goes in v2:
time: 49.5 us; the launch traced here: 49.3 us
  Pallas kernels  44.9 us (91%)
  local copies, waits for them, and re-layouts  3.76 us (8%)
  between operations  0.64 us (1%)
    pallas_call x1, Pallas kernels, body(): pl.pallas_call(functools.partial(kernel, nc, nk), out_shape=(jax.ShapeDty...  44.9 us
    unnamed x2, local copies, waits for them, and re-layouts  3.76 us

profile of v2, /device:TPU:0, one launch (start us, length us, event | category | flops | bytes accessed | tf_op | source)
XLA Modules:
  0.0 49.3 jit_solution(12540550488092213200)
XLA Ops:
  0.6 44.9 %shard_map.86 = (bf16[16,64,256]{2,1,0:T(8,128)(2,1)}, bf16[16,64,256]{2,1,0:T(8,128)(2,1)}) custom-call(bf16[16,64,256]{2,1,0:T(8,128)(2,1)} %density_hbm.1, s32[16,9]{1,0:T(8,128)} %near_hbm.1, s32[2,27]{1,0:T(2,128)} %far_hbm.1, bf16[16,9,64,128]{3,2,1,0:T(8,128)(2,1)} %nb_hbm.1, bf16[16,64,64]{2,1,0:T(8,128)(2,1)} %basis_hbm.1, ...), custom_call_target="tpu_custom_call" | custom-call | flops 1207959552 | bytes 2359296 | tf_op jit(solution)/shard_map/pallas_call | solution.py:333
  45.6 1.9 %copy.11 = bf16[16,64,256]{2,1,0:T(8,128)(2,1)} copy(bf16[16,64,256]{2,1,0:T(8,128)(2,1)} %get-tuple-element.4) | data formatting | bytes 1048576
  47.4 1.9 %copy.12 = bf16[16,64,256]{2,1,0:T(8,128)(2,1)} copy(bf16[16,64,256]{2,1,0:T(8,128)(2,1)} %get-tuple-element.5) | data formatting | bytes 1048576
